TPU v7x, 32 devices: a whole 2x2x4 slice. The times are simulated.
32 devices in a mesh: wide: 8 (over z, y), rep: 4 (over x, core).
Axes of the slice: x: 2, y: 2, z: 4, core: 2. Of those that a mesh axis runs over, the one named last changes fastest.
Arguments:
- integrals: float32 [8, 1, 512, 512], P('wide', None, 'rep'), may hold values from -0.25 to 0.25
- driver: float32 [8, 256, 1, 512], P(None, 'wide', None, 'rep'), may hold values from -12 to 12
- occ_energy: float32 [8, 256], P(None, 'wide'), may hold values from -2 to -0.5
- vir_energy: float32 [8, 1, 512], P(None, None, 'rep'), may hold values from 1 to 8
- occ_count: int32 [8], replicated, may hold values from 64 to 256, as said below
- tile_width: int32 [8, 1], replicated, may hold values from 128 to 512, as said below
Outputs:
- amplitudes: float32 [8, 256, 1, 512], P(None, 'wide', None, 'rep')
Inputs may be any that keep to these rules, and one draw needn't show every extreme that they name: `occ_count`: some pair irrep has all 256 rows live and some has 64. `tile_width`: some tile is fully live and some has 128 live pairs.
All inputs are finite; a program needn't handle non-finite values.
Results may differ from a plain program's by a relative error of at most 0.0001.
Values sent between devices are 32-bit elements; how exact they have to be, the bound alone decides.
A program may use at most 128 MiB of HBM per device.

v0:
```python
import jax
import jax.numpy as jnp
from jax import lax
from jax.sharding import PartitionSpec as P

ITERS = 2


def shards(integrals, driver, occ_energy, vir_energy, occ_count, tile_width):
    n_wide = lax.axis_size("wide")
    wide_index = lax.axis_index("wide")
    rep_index = lax.axis_index("rep")
    groups = driver.shape[0]
    row_count = driver.shape[1]
    tile_count = driver.shape[2]
    quarter = driver.shape[3]
    out_width = integrals.shape[3]
    all_rows = row_count * n_wide
    row_ids = wide_index * row_count + jnp.arange(row_count, dtype=jnp.int32)
    col_ids = rep_index * quarter + jnp.arange(quarter, dtype=jnp.int32)
    rows_live = row_ids[None, :] < occ_count[:, None]
    cols_live = col_ids[None, None, :] < tile_width[:, :, None]
    live_mask = (rows_live[:, :, None, None] & cols_live[:, None, :, :]).astype(jnp.float32)
    weighting = live_mask / (vir_energy[:, None, :, :] - occ_energy[:, :, None, None])
    amplitudes = driver * weighting
    weights = integrals.reshape(tile_count * quarter, out_width)
    for sweep in range(ITERS):

        def add_tile(tile_index, running):
            tile_piece = lax.dynamic_index_in_dim(amplitudes, tile_index, 2, keepdims=False)
            outgoing = jnp.broadcast_to(
                tile_piece[:, None], (groups, n_wide // groups, row_count, quarter)
            )
            outgoing = outgoing.reshape(n_wide, row_count, quarter)
            received = lax.all_to_all(outgoing, "wide", split_axis=0, concat_axis=1, tiled=True)
            tile_rows = received.reshape(all_rows, quarter)
            tile_slice = lax.dynamic_slice_in_dim(weights, tile_index * quarter, quarter, 0)
            return running + jnp.dot(
                tile_rows,
                tile_slice,
                precision=lax.Precision.HIGHEST,
                preferred_element_type=jnp.float32,
            )

        partial_value = lax.fori_loop(
            0, tile_count, add_tile, jnp.zeros((all_rows, out_width), jnp.float32)
        )
        returned = lax.all_to_all(
            partial_value.reshape(1, all_rows, out_width),
            "wide",
            split_axis=1,
            concat_axis=0,
            tiled=True,
        )
        returned = returned.reshape(groups, tile_count, row_count, out_width)
        reduced = lax.psum_scatter(returned, "rep", scatter_dimension=3, tiled=True)
        amplitudes = (driver + jnp.transpose(reduced, (0, 2, 1, 3))) * weighting
    return amplitudes


def solution(mesh):
    placed = (
        P("wide", None, "rep", None),
        P(None, "wide", None, "rep"),
        P(None, "wide"),
        P(None, None, "rep"),
        P(),
        P(),
    )
    return jax.shard_map(
        shards, mesh=mesh, in_specs=placed, out_specs=P(None, "wide", None, "rep"), check_vma=False
    )
```

profile of v0, /device:TPU:0, one launch (start us, length us, event | category | flops | bytes accessed | tf_op | source)
XLA Modules:
  0.0 123.6 jit_solution(17928891614889767990)
XLA Ops:
  6.6 0.0 copy-start.5
  6.6 0.0 copy-start.3
  6.6 0.7 copy-done.4
  7.2 0.1 broadcast_compare_fusion.1
  7.3 0.1 broadcast_compare_fusion
  7.4 0.5 copy-done.2
  7.9 1.6 %fusion.3 = f32[8,32,1,128]{3,2,1,0:T(1,128)S(1)} fusion(f32[8,32,1,128]{3,2,1,0:T(1,128)} %param.7, f32[8,32]{1,0:T(8,128)S(1)} %copy-done.2, f32[8,128]{1,0:T(8,128)S(1)} %bitcast.29, pred[8,128]{1,0:T(8,128)(4,1)S(1)} %broadcast_compare_fusion, pred[8,32]{1,0:T(8,128)(4,1)S(1)} %broadcast_compare_fusion.1), kind=kLoop, calls=%fused_computation.12 | loop fusion | flops 163840 | bytes 268544 | tf_op jit(solution)/shard_map/mul | solution.py:25
  9.5 14.4 %all_to_all.44 = f32[8,32,128]{2,1,0:T(8,128)S(1)} all-to-all(f32[8,32,128]{2,1,0:T(8,128)S(1)} %bitcast.26), channel_id=1, replica_groups=mesh['wide'=8,'rep'=4] {'wide'}, dimensions={0} | all-to-all | bytes 262144 | tf_op jit(solution)/shard_map/while/body/eval_jaxpr/all_to_all | solution.py:35
  23.9 0.6 convolution_bitcast_fusion.1
  24.5 0.5 copy.7
  25.1 15.8 %all_to_all.45 = f32[1,256,512]{2,0,1:T(1,128)S(1)} all-to-all(f32[1,256,512]{2,0,1:T(1,128)S(1)} %copy.7), channel_id=1, replica_groups=mesh['wide'=8,'rep'=4] {'wide'}, dimensions={1} | all-to-all | bytes 1048576 | tf_op jit(solution)/shard_map/all_to_all | solution.py:48
  40.8 0.8 copy.8
  41.7 0.0 reduce-scatter.3.cloned.1.call-update
  41.7 0.0 reduce-scatter.5.cloned.1.call-start
  41.7 20.8 %reduce-scatter.3.cloned.1.call-done = f32[8,1,32,128]{3,2,0,1:T(8,128)} async-done(((f32[8,1,32,512]{3,2,0,1:T(8,128)}), f32[8,1,32,128]{3,2,0,1:T(8,128)}) %reduce-scatter.3.cloned.1.call-update) | async-done | bytes 131088 | tf_op jit(solution)/shard_map/reduce_scatter | solution.py:56
  62.5 1.6 %add_multiply_fusion.1 = f32[8,32,1,128]{3,2,1,0:T(1,128)S(1)} fusion(f32[8,32,1,128]{3,2,1,0:T(1,128)S(1)} %copy-done.1, f32[8,32,1,128]{3,2,1,0:T(1,128)} %bitcast.27, f32[8,32]{1,0:T(8,128)S(1)} %copy-done.2, f32[8,128]{1,0:T(8,128)S(1)} %bitcast.30, pred[8,128]{1,0:T(8,128)(4,1)S(1)} %broadcast_compare_fusion, pred[8,32]{1,0:T(8,128)(4,1)S(1)} %broadcast_compare_fusion.1), kind=kLoop, calls=%fused_computation.7 | loop fusion | flops 196608 | bytes 399616 | tf_op jit(solution)/shard_map/mul | solution.py:57
  64.1 12.7 %all_to_all.46 = f32[8,32,128]{2,1,0:T(8,128)S(1)} all-to-all(f32[8,32,128]{2,1,0:T(8,128)S(1)} %bitcast.24), channel_id=1, replica_groups=mesh['wide'=8,'rep'=4] {'wide'}, dimensions={0} | all-to-all | bytes 262144 | tf_op jit(solution)/shard_map/while/body/eval_jaxpr/all_to_all | solution.py:35
  76.8 0.6 convolution_bitcast_fusion
  77.4 0.5 copy.9
  77.9 15.8 %all_to_all.47 = f32[1,256,512]{2,0,1:T(1,128)S(1)} all-to-all(f32[1,256,512]{2,0,1:T(1,128)S(1)} %copy.9), channel_id=1, replica_groups=mesh['wide'=8,'rep'=4] {'wide'}, dimensions={1} | all-to-all | bytes 1048576 | tf_op jit(solution)/shard_map/all_to_all | solution.py:48
  93.7 0.8 copy.10
  94.6 0.0 reduce-scatter.5.cloned.1.call-update
  94.6 20.0 %reduce-scatter.5.cloned.1.call-done = f32[8,1,32,128]{3,2,0,1:T(8,128)} async-done(((f32[8,1,32,512]{3,2,0,1:T(8,128)}), f32[8,1,32,128]{3,2,0,1:T(8,128)}) %reduce-scatter.5.cloned.1.call-update) | async-done | bytes 131088 | tf_op jit(solution)/shard_map/reduce_scatter | solution.py:56
  114.6 2.2 %add_multiply_fusion = f32[8,32,1,128]{3,2,1,0:T(1,128)} fusion(f32[8,32,1,128]{3,2,1,0:T(1,128)S(1)} %copy-done.1, f32[8,32,1,128]{3,2,1,0:T(1,128)} %bitcast.28, f32[8,32]{1,0:T(8,128)S(1)} %copy-done.2, f32[8,128]{1,0:T(8,128)S(1)} %bitcast.31, pred[8,128]{1,0:T(8,128)(4,1)S(1)} %broadcast_compare_fusion, pred[8,32]{1,0:T(8,128)(4,1)S(1)} %broadcast_compare_fusion.1), kind=kLoop, calls=%fused_computation.6 | loop fusion | flops 196608 | bytes 399616 | tf_op jit(solution)/shard_map/mul | solution.py:57
  (11 shorter events, 0.0 us)
Async XLA Ops:
  6.5 17.4 %copy-start = (f32[1,1,128,512]{3,2,1,0:T(8,128)S(1)}, f32[1,1,128,512]{3,2,1,0:T(8,128)}, u32[]{:S(2)}) copy-start(f32[1,1,128,512]{3,2,1,0:T(8,128)} %param.6) | copy-start | bytes 786436
  6.5 56.0 %reduce-scatter.3.cloned.1.call-start = ((), (), s32[]{:S(2)}) async-start(), calls=%async_computation.6 | async-start | bytes 655360 | tf_op jit(solution)/shard_map/reduce_scatter | solution.py:56
  6.5 0.7 copy-start.4
  6.6 0.8 copy-start.5
  6.6 0.8 copy-start.3
  7.2 0.7 copy-start.2
  41.7 20.9 %copy-start.1 = (f32[8,32,1,128]{3,2,1,0:T(1,128)S(1)}, f32[8,32,1,128]{3,2,1,0:T(1,128)}, u32[]{:S(2)}) copy-start(f32[8,32,1,128]{3,2,1,0:T(1,128)} %param.7) | copy-start | bytes 393220
  41.7 72.9 %reduce-scatter.5.cloned.1.call-start = ((), (), s32[]{:S(2)}) async-start(), calls=%async_computation.7 | async-start | bytes 655360 | tf_op jit(solution)/shard_map/reduce_scatter | solution.py:56
Sparse Core Ops, SparseCore 0:
  41.8 20.6 reduce-scatter.2
  94.7 19.7 reduce-scatter.4
where the time goes:
time: 124 us
  blocking collectives  58.7 us (47%)
  waiting for transfers between devices  40.8 us (33%)
  between operations  13.5 us (11%)
  other arithmetic  5.46 us (4%)
  local copies, waits for them, and re-layouts  3.98 us (3%)
    reduce_scatter x2, waiting for transfers between devices, shards(): reduced = lax.psum_scatter(returned, 'rep', scatter_dimension=3, tiled=True)  40.8 us
    all_to_all x2, blocking collectives, shards(): lax.all_to_all(partial_value.reshape(1, all_rows, out_width), 'wide', spl...  31.6 us
    all_to_all x2, blocking collectives, add_tile(): lax.all_to_all(outgoing, 'wide', split_axis=0, concat_axis=1, tiled=True)  27.1 us
    mul x2, other arithmetic, shards(): amplitudes = (driver + jnp.transpose(reduced, (0, 2, 1, 3))) * weighting  3.74 us
  transfers between devices with their start and end apart: 2, of which 2 were waited for; matrix products, arithmetic and copies ran while one was open for 0% of the time, Pallas kernels for 0%

commit v1 on v0

--- a/solution.py
+++ b/solution.py
@@ -1,12 +1,271 @@
+import functools
+
 import jax
 import jax.numpy as jnp
 from jax import lax
+from jax.experimental import pallas as pl
+from jax.experimental.pallas import tpu as pltpu
 from jax.sharding import PartitionSpec as P
 
 ITERS = 2
-
-
-def shards(integrals, driver, occ_energy, vir_energy, occ_count, tile_width):
+MESH = pl.DeviceIdType.MESH
+F32 = jnp.float32
+BF16 = jnp.bfloat16
+
+
+def split(value):
+    high = value.astype(BF16)
+    low = (value - high.astype(F32)).astype(BF16)
+    return high, low
+
+
+def product(high, low, weight_high, weight_low):
+    dot = functools.partial(jnp.dot, preferred_element_type=F32)
+    return dot(high, weight_high) + (dot(low, weight_high) + dot(high, weight_low))
+
+
+def ladder_kernel(
+    n_wide, n_rep, chunks,
+    count_ref, width_ref, v_ref, d_ref, occ_ref, vir_ref, out_ref,
+    v_all, v_high, v_low, d_all, a_high, a_low, e_src, e_all, vir_src, vir_all, stage,
+    chip_send, chip_recv, pair_send, pair_recv, relay_send, relay_recv,
+    d_send, d_recv, e_send, e_recv, vir_send, vir_recv, out_send, out_recv,
+):
+    wide = lax.axis_index("wide")
+    rep = lax.axis_index("rep")
+    total = n_wide * n_rep
+    me = wide * n_rep + rep
+    depth, width = v_ref.shape
+    sub = 8
+    row_count = sub * n_rep
+    rows = n_wide * sub
+    half = lax.div(rep, 2)
+    pair = rep + 1 - 2 * lax.rem(rep, 2)
+    mirror = lax.rem(rep + 2, n_rep)
+    piece = depth // chunks
+
+    barrier = pltpu.get_barrier_semaphore()
+
+    def greet(step, carry):
+        other = lax.rem(me + step, total)
+        pl.semaphore_signal(
+            barrier, inc=1, device_id=(lax.div(other, n_rep), lax.rem(other, n_rep)), device_id_type=MESH
+        )
+        return carry
+
+    lax.fori_loop(1, total, greet, 0)
+
+    lane = lax.broadcasted_iota(jnp.int32, (sub, row_count), 1)
+    sublane = lax.broadcasted_iota(jnp.int32, (sub, row_count), 0)
+    pick = lane == sublane + rep * sub
+    for group in range(n_wide):
+        row = jnp.broadcast_to(occ_ref[group:group + 1, :], (sub, row_count))
+        column = jnp.sum(jnp.where(pick, row, 0.0), axis=1, keepdims=True)
+        e_src[group] = jnp.broadcast_to(column, (sub, 128))
+    vir_src[...] = jnp.broadcast_to(vir_ref[pl.ds(wide, 1), :], vir_src.shape)
+
+    pl.semaphore_wait(barrier, total - 1)
+
+    chip_copies = []
+    for chunk in range(chunks):
+        span = pl.ds(chunk * piece, piece)
+        copy = pltpu.make_async_remote_copy(
+            src_ref=v_ref.at[span], dst_ref=v_all.at[rep, span],
+            send_sem=chip_send.at[chunk], recv_sem=chip_recv.at[chunk],
+            device_id=(wide, mirror), device_id_type=MESH,
+        )
+        copy.start()
+        chip_copies.append(copy)
+    pair_copy = pltpu.make_async_remote_copy(
+        src_ref=v_ref, dst_ref=v_all.at[rep], send_sem=pair_send, recv_sem=pair_recv,
+        device_id=(wide, pair), device_id_type=MESH,
+    )
+    pair_copy.start()
+
+    def send_driver(step, carry):
+        other = lax.rem(me + step, total)
+        group = lax.div(other, n_rep)
+        share = lax.rem(other, n_rep)
+        pltpu.make_async_remote_copy(
+            src_ref=d_ref.at[pl.ds(pl.multiple_of(group * row_count + share * sub, sub), sub)],
+            dst_ref=d_all.at[rep, pl.ds(pl.multiple_of(wide * sub, sub), sub)],
+            send_sem=d_send, recv_sem=d_recv,
+            device_id=(group, share), device_id_type=MESH,
+        ).start()
+        return carry
+
+    lax.fori_loop(1, total, send_driver, 0)
+    pltpu.make_async_copy(
+        d_ref.at[pl.ds(pl.multiple_of(wide * row_count + rep * sub, sub), sub)],
+        d_all.at[rep, pl.ds(pl.multiple_of(wide * sub, sub), sub)],
+        d_recv,
+    ).start()
+    for step in range(1, n_rep):
+        pltpu.make_async_remote_copy(
+            src_ref=vir_src, dst_ref=vir_all.at[rep], send_sem=vir_send, recv_sem=vir_recv,
+            device_id=(wide, lax.rem(rep + step, n_rep)), device_id_type=MESH,
+        ).start()
+    pltpu.make_async_copy(vir_src, vir_all.at[rep], vir_recv).start()
+    for step in range(1, n_wide):
+        group = lax.rem(wide + step, n_wide)
+        pltpu.make_async_remote_copy(
+            src_ref=e_src.at[group], dst_ref=e_all.at[wide], send_sem=e_send, recv_sem=e_recv,
+            device_id=(group, rep), device_id_type=MESH,
+        ).start()
+    pltpu.make_async_copy(e_src.at[wide], e_all.at[wide], e_recv).start()
+
+    def hold(block, value):
+        high, low = split(value)
+        v_high[block] = high
+        v_low[block] = low
+
+    hold(rep, v_ref[...])
+    pair_copy.wait_recv()
+    hold(pair, v_all[pair])
+
+    pltpu.make_async_copy(e_all, e_all, e_recv).wait()
+    pltpu.make_async_copy(vir_all, vir_all, vir_recv).wait()
+    pltpu.make_async_copy(d_all, d_all, d_recv).wait()
+
+    count = count_ref[wide]
+    live_width = width_ref[wide]
+    local = lax.broadcasted_iota(jnp.int32, (rows, 128), 0)
+    row_id = lax.div(local, sub) * row_count + rep * sub + lax.rem(local, sub)
+    col_id = lax.broadcasted_iota(jnp.int32, (rows, 128), 1)
+    occ = e_all[...].reshape(rows, 128)
+    weighting = []
+    for block in range(n_rep):
+        live = ((row_id < count) & (col_id + block * depth < live_width)).astype(F32)
+        vir = jnp.broadcast_to(vir_all[block, 0:1, :], (rows, 128))
+        weighting.append(live / (vir - occ))
+    driver = [d_all[block] for block in range(n_rep)]
+    for block in range(n_rep):
+        high, low = split(driver[block] * weighting[block])
+        a_high[block] = high
+        a_low[block] = low
+
+    def half_product(which):
+        first = 2 * which
+        return product(
+            jnp.concatenate([a_high[first], a_high[first + 1]], axis=1),
+            jnp.concatenate([a_low[first], a_low[first + 1]], axis=1),
+            v_high[pl.ds(first, 2)].reshape(2 * depth, width),
+            v_low[pl.ds(first, 2)].reshape(2 * depth, width),
+        )
+
+    ladder = half_product(half)
+
+    relays = []
+    for chunk in range(chunks):
+        span = pl.ds(chunk * piece, piece)
+        chip_copies[chunk].wait_recv()
+        relay = pltpu.make_async_remote_copy(
+            src_ref=v_all.at[mirror, span], dst_ref=v_all.at[mirror, span],
+            send_sem=relay_send.at[chunk], recv_sem=relay_recv.at[chunk],
+            device_id=(wide, pair), device_id_type=MESH,
+        )
+        relay.start()
+        relays.append(relay)
+    hold(mirror, v_all[mirror])
+    for relay in relays:
+        relay.wait_recv()
+    far = lax.rem(pair + 2, n_rep)
+    hold(far, v_all[far])
+    ladder = ladder + half_product(1 - half)
+
+    for sweep in range(1, ITERS):
+        for block in range(n_rep):
+            part = ladder[:, block * depth:(block + 1) * depth]
+            high, low = split((driver[block] + part) * weighting[block])
+            a_high[block] = high
+            a_low[block] = low
+        ladder = half_product(0) + half_product(1)
+    for block in range(n_rep):
+        part = ladder[:, block * depth:(block + 1) * depth]
+        stage[block] = (driver[block] + part) * weighting[block]
+
+    def send_out(step, carry):
+        other = lax.rem(me + step, total)
+        owner = lax.div(other, n_rep)
+        block = lax.rem(other, n_rep)
+        pltpu.make_async_remote_copy(
+            src_ref=stage.at[block, pl.ds(pl.multiple_of(owner * sub, sub), sub)],
+            dst_ref=out_ref.at[pl.ds(pl.multiple_of(wide * row_count + rep * sub, sub), sub)],
+            send_sem=out_send, recv_sem=out_recv,
+            device_id=(owner, block), device_id_type=MESH,
+        ).start()
+        return carry
+
+    lax.fori_loop(1, total, send_out, 0)
+    pltpu.make_async_copy(
+        stage.at[rep, pl.ds(pl.multiple_of(wide * sub, sub), sub)],
+        out_ref.at[pl.ds(pl.multiple_of(wide * row_count + rep * sub, sub), sub)],
+        out_recv,
+    ).start()
+
+    for copy in chip_copies:
+        copy.wait_send()
+    pair_copy.wait_send()
+    for relay in relays:
+        relay.wait_send()
+    sent = d_ref.at[pl.ds(0, (total - 1) * sub)]
+    pltpu.make_async_copy(sent, sent, d_send).wait()
+    sent = e_src.at[pl.ds(0, n_wide - 1)]
+    pltpu.make_async_copy(sent, sent, e_send).wait()
+    sent = vir_all.at[pl.ds(0, n_rep - 1)]
+    pltpu.make_async_copy(sent, sent, vir_send).wait()
+    sent = d_ref.at[pl.ds(0, (total - 1) * sub)]
+    pltpu.make_async_copy(sent, sent, out_send).wait()
+    pltpu.make_async_copy(out_ref, out_ref, out_recv).wait()
+
+
+def group_shards(integrals, driver, occ_energy, vir_energy, occ_count, tile_width):
+    n_wide = lax.axis_size("wide")
+    n_rep = lax.axis_size("rep")
+    groups, row_count, _, depth = driver.shape
+    width = integrals.shape[3]
+    sub = row_count // n_rep
+    rows = n_wide * sub
+    chunks = 4
+    vmem = pl.BlockSpec(memory_space=pltpu.VMEM)
+    smem = pl.BlockSpec(memory_space=pltpu.SMEM)
+    dma = pltpu.SemaphoreType.DMA
+    out = pl.pallas_call(
+        functools.partial(ladder_kernel, n_wide, n_rep, chunks),
+        out_shape=jax.ShapeDtypeStruct((groups * row_count, depth), F32),
+        in_specs=[smem, smem, vmem, vmem, vmem, vmem],
+        out_specs=vmem,
+        scratch_shapes=[
+            pltpu.VMEM((n_rep, depth, width), F32),
+            pltpu.VMEM((n_rep, depth, width), BF16),
+            pltpu.VMEM((n_rep, depth, width), BF16),
+            pltpu.VMEM((n_rep, rows, depth), F32),
+            pltpu.VMEM((n_rep, rows, depth), BF16),
+            pltpu.VMEM((n_rep, rows, depth), BF16),
+            pltpu.VMEM((n_wide, sub, 128), F32),
+            pltpu.VMEM((n_wide, sub, 128), F32),
+            pltpu.VMEM((8, 128), F32),
+            pltpu.VMEM((n_rep, 8, 128), F32),
+            pltpu.VMEM((n_rep, rows, depth), F32),
+            dma((chunks,)), dma((chunks,)), dma, dma, dma((chunks,)), dma((chunks,)),
+            dma, dma, dma, dma, dma, dma, dma, dma,
+        ],
+        compiler_params=pltpu.CompilerParams(
+            collective_id=0, has_side_effects=True, vmem_limit_bytes=32 * 1024 * 1024
+        ),
+        name="ladder_sweeps",
+    )(
+        occ_count,
+        tile_width.reshape(groups),
+        integrals.reshape(depth, width),
+        driver.reshape(groups * row_count, depth),
+        occ_energy,
+        vir_energy.reshape(groups, depth),
+    )
+    return out.reshape(groups, row_count, 1, depth)
+
+
+def tiled_shards(integrals, driver, occ_energy, vir_energy, occ_count, tile_width):
     n_wide = lax.axis_size("wide")
     wide_index = lax.axis_index("wide")
     rep_index = lax.axis_index("rep")
@@ -45,17 +304,26 @@
         partial_value = lax.fori_loop(
             0, tile_count, add_tile, jnp.zeros((all_rows, out_width), jnp.float32)
         )
+        reduced = lax.psum_scatter(partial_value, "rep", scatter_dimension=1, tiled=True)
         returned = lax.all_to_all(
-            partial_value.reshape(1, all_rows, out_width),
+            reduced.reshape(1, all_rows, quarter),
             "wide",
             split_axis=1,
             concat_axis=0,
             tiled=True,
         )
-        returned = returned.reshape(groups, tile_count, row_count, out_width)
-        reduced = lax.psum_scatter(returned, "rep", scatter_dimension=3, tiled=True)
-        amplitudes = (driver + jnp.transpose(reduced, (0, 2, 1, 3))) * weighting
+        returned = returned.reshape(groups, tile_count, row_count, quarter)
+        amplitudes = (driver + jnp.transpose(returned, (0, 2, 1, 3))) * weighting
     return amplitudes
+
+
+def shards(integrals, driver, occ_energy, vir_energy, occ_count, tile_width):
+    n_wide = lax.axis_size("wide")
+    n_rep = lax.axis_size("rep")
+    groups, row_count, tile_count, depth = driver.shape
+    fits = tile_count == 1 and groups == n_wide and n_rep == 4 and row_count == 8 * n_rep and depth == 128
+    body = group_shards if fits else tiled_shards
+    return body(integrals, driver, occ_energy, vir_energy, occ_count, tile_width)
 
 
 def solution(mesh):

time: 124 us -> 27.7 us (0.22)
  blocking collectives: 58.7 us -> 0 us
  waiting for transfers between devices: 40.8 us -> 0 us
  Pallas kernels: 0 us -> 23.6 us
  between operations: 13.5 us -> 0.02 us
  other arithmetic: 5.46 us -> 0 us
    all_to_all x4 -> x0, blocking collectives: 58.7 us -> none  [the longest x2 31.6 us: shards(): lax.all_to_all(partial_value.reshape(1, all_rows, out_width), 'wide', spl...]
    reduce_scatter x2 -> x0, waiting for transfers between devices: 40.8 us -> none  [shards(): reduced = lax.psum_scatter(returned, 'rep', scatter_dimension=3, tiled=True)]
    pallas_call x0 -> x1, Pallas kernels: none -> 23.6 us  [group_shards(): pl.pallas_call(functools.partial(ladder_kernel, n_wide, n_rep, chunks), o...]
    mul x3 -> x0, other arithmetic: 5.31 us -> none  [the longest x2 3.74 us: shards(): amplitudes = (driver + jnp.transpose(reduced, (0, 2, 1, 3))) * weighting]
    reshape x4 -> x0, local copies, waits for them, and re-layouts: 2.77 us -> none  [the longest x2 1.69 us: shards(): returned = returned.reshape(groups, tile_count, row_count, out_width)]
    unnamed x12 -> x13, local copies, waits for them, and re-layouts: 1.21 us -> 3.89 us
  transfers between devices with their start and end apart: 2 -> 0, of which waited for: 2 -> 0; matrix products, arithmetic and copies ran while one was open for 0% -> 0% of each run, Pallas kernels for 0% -> 0%
where the time goes in v1:
time: 27.7 us; the launch traced here: 27.5 us
  Pallas kernels  23.6 us (85%)
  local copies, waits for them, and re-layouts  3.89 us (14%)
    pallas_call x1, Pallas kernels, group_shards(): pl.pallas_call(functools.partial(ladder_kernel, n_wide, n_rep, chunks), o...  23.6 us
    unnamed x13, local copies, waits for them, and re-layouts  3.89 us

profile of v1, /device:TPU:0, one launch (start us, length us, event | category | flops | bytes accessed | tf_op | source)
XLA Modules:
  0.0 27.5 jit_solution(12018186851031524836)
XLA Ops:
  0.0 0.0 copy-start.2
  0.0 0.0 copy-start.4
  0.0 0.0 copy-start.5
  0.0 0.7 %copy-done.2 = f32[8,32]{1,0:T(8,128)S(1)} copy-done((f32[8,32]{1,0:T(8,128)S(1)}, f32[8,32]{1,0:T(8,128)}, u32[]{:S(2)}) %copy-start.2) | copy-done | bytes 1048
  0.7 0.0 copy-done.4
  0.7 0.0 copy-done.5
  0.7 0.0 copy-start
  0.7 0.9 %copy-done = f32[1,1,128,512]{3,2,1,0:T(8,128)S(1)} copy-done((f32[1,1,128,512]{3,2,1,0:T(8,128)S(1)}, f32[1,1,128,512]{3,2,1,0:T(8,128)}, u32[]{:S(2)}) %copy-start) | copy-done | bytes 262168
  1.6 0.0 copy-start.1
  1.6 0.9 %copy-done.1 = f32[8,32,1,128]{3,2,1,0:T(1,128)S(1)} copy-done((f32[8,32,1,128]{3,2,1,0:T(1,128)S(1)}, f32[8,32,1,128]{3,2,1,0:T(1,128)}, u32[]{:S(2)}) %copy-start.1) | copy-done | bytes 131096
  2.5 0.0 copy-start.3
  2.6 0.7 %copy-done.3 = f32[8,1,128]{2,1,0:T(1,128)S(1)} copy-done((f32[8,1,128]{2,1,0:T(1,128)S(1)}, f32[8,1,128]{2,1,0:T(1,128)}, u32[]{:S(2)}) %copy-start.3) | copy-done | bytes 4120
  3.2 23.6 %ladder_sweeps.1 = f32[256,128]{1,0:T(8,128)S(1)} custom-call(s32[8]{0:T(128)S(1)} %copy-done.4, s32[8]{0:T(128)S(1)} %bitcast.11, f32[128,512]{1,0:T(8,128)S(1)} %bitcast.8, f32[256,128]{1,0:T(8,128)S(1)} %bitcast.9, f32[8,32]{1,0:T(8,128)S(1)} %copy-done.2, f32[8,128]{1,0:T(8,128)S(1)} %bitcast.10), custom_call_target="tpu_custom_call" | custom-call | tf_op jit(solution)/shard_map/ladder_sweeps/pallas_call | solution.py:233
  26.8 0.7 %copy.9 = f32[8,32,1,128]{3,2,1,0:T(1,128)} copy(f32[8,32,1,128]{3,2,1,0:T(1,128)S(1)} %bitcast.7) | data formatting | bytes 262144
Async XLA Ops:
  0.0 0.7 %copy-start.2 = (f32[8,32]{1,0:T(8,128)S(1)}, f32[8,32]{1,0:T(8,128)}, u32[]{:S(2)}) copy-start(f32[8,32]{1,0:T(8,128)} %occ_ref.1) | copy-start | bytes 3076
  0.0 0.7 %copy-start.4 = (s32[8]{0:T(128)S(1)}, s32[8]{0:T(128)}, u32[]{:S(2)}) copy-start(s32[8]{0:T(128)} %count_ref.1) | copy-start | bytes 100
  0.0 0.7 %copy-start.5 = (s32[8,1]{0,1:T(1,128)S(1)}, s32[8,1]{0,1:T(1,128)}, u32[]{:S(2)}) copy-start(s32[8,1]{0,1:T(1,128)} %param.11) | copy-start | bytes 100
  0.7 1.0 %copy-start = (f32[1,1,128,512]{3,2,1,0:T(8,128)S(1)}, f32[1,1,128,512]{3,2,1,0:T(8,128)}, u32[]{:S(2)}) copy-start(f32[1,1,128,512]{3,2,1,0:T(8,128)} %param.6) | copy-start | bytes 786436
  1.6 0.9 %copy-start.1 = (f32[8,32,1,128]{3,2,1,0:T(1,128)S(1)}, f32[8,32,1,128]{3,2,1,0:T(1,128)}, u32[]{:S(2)}) copy-start(f32[8,32,1,128]{3,2,1,0:T(1,128)} %param.7) | copy-start | bytes 393220
  2.5 0.7 %copy-start.3 = (f32[8,1,128]{2,1,0:T(1,128)S(1)}, f32[8,1,128]{2,1,0:T(1,128)}, u32[]{:S(2)}) copy-start(f32[8,1,128]{2,1,0:T(1,128)} %param.9) | copy-start | bytes 12292

commit v2 on v1

--- a/solution.py
+++ b/solution.py
@@ -26,8 +26,8 @@
 
 def ladder_kernel(
     n_wide, n_rep, chunks,
-    count_ref, width_ref, v_ref, d_ref, occ_ref, vir_ref, out_ref,
-    v_all, v_high, v_low, d_all, a_high, a_low, e_src, e_all, vir_src, vir_all, stage,
+    count_in, width_in, v_ref, d_ref, occ_in, vir_in, out_ref,
+    count_ref, width_ref, occ_ref, vir_ref, load_sem, v_load, v_all, v_high, v_low, d_all, a_high, a_low, e_src, e_all, vir_src, vir_all, stage,
     chip_send, chip_recv, pair_send, pair_recv, relay_send, relay_recv,
     d_send, d_recv, e_send, e_recv, vir_send, vir_recv, out_send, out_recv,
 ):
@@ -54,6 +54,19 @@
         return carry
 
     lax.fori_loop(1, total, greet, 0)
+
+    loads = [
+        pltpu.make_async_copy(occ_in, occ_ref, load_sem.at[0]),
+        pltpu.make_async_copy(vir_in, vir_ref, load_sem.at[1]),
+        pltpu.make_async_copy(count_in, count_ref, load_sem.at[2]),
+        pltpu.make_async_copy(width_in, width_ref, load_sem.at[3]),
+    ]
+    own_load = pltpu.make_async_copy(v_ref, v_all.at[rep], v_load)
+    for load in loads:
+        load.start()
+    own_load.start()
+    for load in loads:
+        load.wait()
 
     lane = lax.broadcasted_iota(jnp.int32, (sub, row_count), 1)
     sublane = lax.broadcasted_iota(jnp.int32, (sub, row_count), 0)
@@ -119,7 +132,8 @@
         v_high[block] = high
         v_low[block] = low
 
-    hold(rep, v_ref[...])
+    own_load.wait()
+    hold(rep, v_all[rep])
     pair_copy.wait_recv()
     hold(pair, v_all[pair])
 
@@ -228,14 +242,18 @@
     rows = n_wide * sub
     chunks = 4
     vmem = pl.BlockSpec(memory_space=pltpu.VMEM)
-    smem = pl.BlockSpec(memory_space=pltpu.SMEM)
     dma = pltpu.SemaphoreType.DMA
     out = pl.pallas_call(
         functools.partial(ladder_kernel, n_wide, n_rep, chunks),
-        out_shape=jax.ShapeDtypeStruct((groups * row_count, depth), F32),
-        in_specs=[smem, smem, vmem, vmem, vmem, vmem],
+        out_shape=pltpu.VMEM((groups * row_count, depth), F32),
+        in_specs=[pl.BlockSpec(memory_space=pltpu.HBM)] * 6,
         out_specs=vmem,
         scratch_shapes=[
+            pltpu.SMEM((groups,), jnp.int32),
+            pltpu.SMEM((groups,), jnp.int32),
+            pltpu.VMEM(occ_energy.shape, F32),
+            pltpu.VMEM((groups, depth), F32),
+            dma((4,)), dma,
             pltpu.VMEM((n_rep, depth, width), F32),
             pltpu.VMEM((n_rep, depth, width), BF16),
             pltpu.VMEM((n_rep, depth, width), BF16),
@@ -251,7 +269,7 @@
             dma, dma, dma, dma, dma, dma, dma, dma,
         ],
         compiler_params=pltpu.CompilerParams(
-            collective_id=0, has_side_effects=True, vmem_limit_bytes=32 * 1024 * 1024
+            collective_id=0, has_side_effects=True, vmem_limit_bytes=60 * 1024 * 1024
         ),
         name="ladder_sweeps",
     )(

time: 27.7 us -> 24 us (0.87)
  local copies, waits for them, and re-layouts: 3.89 us -> 0.66 us
  Pallas kernels: 23.6 us -> 23.1 us
    unnamed x13 -> x1, local copies, waits for them, and re-layouts: 3.89 us -> 0.66 us
    pallas_call x1, Pallas kernels: 23.6 us -> 23.1 us  [group_shards(): pl.pallas_call(functools.partial(ladder_kernel, n_wide, n_rep, chunks), o...]
where the time goes in v2:
time: 24 us; the launch traced here: 23.8 us
  Pallas kernels  23.1 us (96%)
  local copies, waits for them, and re-layouts  0.66 us (3%)
    pallas_call x1, Pallas kernels, group_shards(): pl.pallas_call(functools.partial(ladder_kernel, n_wide, n_rep, chunks), o...  23.1 us
    unnamed x1, local copies, waits for them, and re-layouts  0.66 us

profile of v2, /device:TPU:0, one launch (start us, length us, event | category | flops | bytes accessed | tf_op | source)
XLA Modules:
  0.0 23.8 jit_solution(4544437611595423633)
XLA Ops:
  0.0 23.1 %ladder_sweeps.1 = f32[256,128]{1,0:T(8,128)S(1)} custom-call(s32[8]{0:T(128)} %count_in.1, s32[8]{0:T(128)} %bitcast.11, f32[128,512]{1,0:T(8,128)} %bitcast.8, f32[256,128]{1,0:T(8,128)} %bitcast.9, f32[8,32]{1,0:T(8,128)} %occ_in.1, f32[8,128]{1,0:T(8,128)} %bitcast.10), custom_call_target="tpu_custom_call" | custom-call | tf_op jit(solution)/shard_map/ladder_sweeps/pallas_call | solution.py:246
  23.2 0.7 %copy.9 = f32[8,32,1,128]{3,2,1,0:T(1,128)} copy(f32[8,32,1,128]{3,2,1,0:T(1,128)S(1)} %bitcast.7) | data formatting | bytes 262144

commit v3 on v2

--- a/solution.py
+++ b/solution.py
@@ -8,6 +8,7 @@
 from jax.sharding import PartitionSpec as P
 
 ITERS = 2
+PLANE = 2
 MESH = pl.DeviceIdType.MESH
 F32 = jnp.float32
 BF16 = jnp.bfloat16
@@ -28,7 +29,7 @@
     n_wide, n_rep, chunks,
     count_in, width_in, v_ref, d_ref, occ_in, vir_in, out_ref,
     count_ref, width_ref, occ_ref, vir_ref, load_sem, v_load, v_all, v_high, v_low, d_all, a_high, a_low, e_src, e_all, vir_src, vir_all, stage,
-    chip_send, chip_recv, pair_send, pair_recv, relay_send, relay_recv,
+    up_sem, down_sem, chip_send, chip_recv, pair_send, pair_recv, relay_send, relay_recv,
     d_send, d_recv, e_send, e_recv, vir_send, vir_recv, out_send, out_recv,
 ):
     wide = lax.axis_index("wide")
@@ -46,14 +47,27 @@
 
     barrier = pltpu.get_barrier_semaphore()
 
-    def greet(step, carry):
-        other = lax.rem(me + step, total)
-        pl.semaphore_signal(
-            barrier, inc=1, device_id=(lax.div(other, n_rep), lax.rem(other, n_rep)), device_id_type=MESH
-        )
-        return carry
-
-    lax.fori_loop(1, total, greet, 0)
+    plane = lax.div(wide, PLANE)
+    planes = n_wide // PLANE
+    mates = PLANE * n_rep
+    place = me - plane * mates
+    above = (lax.min(wide + PLANE, n_wide - 1), rep)
+    below = (lax.max(wide - PLANE, 0), rep)
+
+    def tell(semaphore, device):
+        pl.semaphore_signal(semaphore, inc=1, device_id=device, device_id_type=MESH)
+
+    for step in range(1, mates):
+        other = plane * mates + lax.rem(place + step, mates)
+        tell(barrier, (lax.div(other, n_rep), lax.rem(other, n_rep)))
+
+    @pl.when(plane < planes - 1)
+    def _():
+        tell(barrier, above)
+
+    @pl.when(plane > 0)
+    def _():
+        tell(barrier, below)
 
     loads = [
         pltpu.make_async_copy(occ_in, occ_ref, load_sem.at[0]),
@@ -77,7 +91,8 @@
         e_src[group] = jnp.broadcast_to(column, (sub, 128))
     vir_src[...] = jnp.broadcast_to(vir_ref[pl.ds(wide, 1), :], vir_src.shape)
 
-    pl.semaphore_wait(barrier, total - 1)
+    beside = jnp.where(plane > 0, 1, 0) + jnp.where(plane < planes - 1, 1, 0)
+    pl.semaphore_wait(barrier, mates - 1 + beside)
 
     chip_copies = []
     for chunk in range(chunks):
@@ -94,6 +109,19 @@
         device_id=(wide, pair), device_id_type=MESH,
     )
     pair_copy.start()
+
+    @pl.when(plane > 0)
+    def _():
+        pl.semaphore_wait(up_sem, 1)
+
+    @pl.when(plane < planes - 1)
+    def _():
+        tell(up_sem, above)
+        pl.semaphore_wait(down_sem, 1)
+
+    @pl.when(plane > 0)
+    def _():
+        tell(down_sem, below)
 
     def send_driver(step, carry):
         other = lax.rem(me + step, total)
@@ -265,6 +293,7 @@
             pltpu.VMEM((8, 128), F32),
             pltpu.VMEM((n_rep, 8, 128), F32),
             pltpu.VMEM((n_rep, rows, depth), F32),
+            pltpu.SemaphoreType.REGULAR, pltpu.SemaphoreType.REGULAR,
             dma((chunks,)), dma((chunks,)), dma, dma, dma((chunks,)), dma((chunks,)),
             dma, dma, dma, dma, dma, dma, dma, dma,
         ],
@@ -339,7 +368,7 @@
     n_wide = lax.axis_size("wide")
     n_rep = lax.axis_size("rep")
     groups, row_count, tile_count, depth = driver.shape
-    fits = tile_count == 1 and groups == n_wide and n_rep == 4 and row_count == 8 * n_rep and depth == 128
+    fits = tile_count == 1 and groups == n_wide and n_wide % PLANE == 0 and n_rep == 4 and row_count == 8 * n_rep and depth == 128
     body = group_shards if fits else tiled_shards
     return body(integrals, driver, occ_energy, vir_energy, occ_count, tile_width)
 

time: 24 us -> 23.2 us (0.967)
  Pallas kernels: 23.1 us -> 22.4 us
    pallas_call x1, Pallas kernels: 23.1 us -> 22.4 us  [group_shards(): pl.pallas_call(functools.partial(ladder_kernel, n_wide, n_rep, chunks), o...]
where the time goes in v3:
time: 23.2 us; the launch traced here: 23 us
  Pallas kernels  22.4 us (97%)
  local copies, waits for them, and re-layouts  0.66 us (3%)
    pallas_call x1, Pallas kernels, group_shards(): pl.pallas_call(functools.partial(ladder_kernel, n_wide, n_rep, chunks), o...  22.4 us
    unnamed x1, local copies, waits for them, and re-layouts  0.66 us

profile of v3, /device:TPU:0, one launch (start us, length us, event | category | flops | bytes accessed | tf_op | source)
XLA Modules:
  0.0 23.0 jit_solution(2135004972000181420)
XLA Ops:
  0.0 22.4 %ladder_sweeps.1 = f32[256,128]{1,0:T(8,128)S(1)} custom-call(s32[8]{0:T(128)} %count_in.1, s32[8]{0:T(128)} %bitcast.11, f32[128,512]{1,0:T(8,128)} %bitcast.8, f32[256,128]{1,0:T(8,128)} %bitcast.9, f32[8,32]{1,0:T(8,128)} %occ_in.1, f32[8,128]{1,0:T(8,128)} %bitcast.10), custom_call_target="tpu_custom_call" | custom-call | tf_op jit(solution)/shard_map/ladder_sweeps/pallas_call | solution.py:274
  22.4 0.7 %copy.9 = f32[8,32,1,128]{3,2,1,0:T(1,128)} copy(f32[8,32,1,128]{3,2,1,0:T(1,128)S(1)} %bitcast.7) | data formatting | bytes 262144

commit v4 on v3

--- a/solution.py
+++ b/solution.py
@@ -186,13 +186,13 @@
         a_high[block] = high
         a_low[block] = low
 
-    def half_product(which):
+    def half_product(which, columns=pl.ds(0, width)):
         first = 2 * which
         return product(
             jnp.concatenate([a_high[first], a_high[first + 1]], axis=1),
             jnp.concatenate([a_low[first], a_low[first + 1]], axis=1),
-            v_high[pl.ds(first, 2)].reshape(2 * depth, width),
-            v_low[pl.ds(first, 2)].reshape(2 * depth, width),
+            v_high[pl.ds(first, 2), :, columns].reshape(2 * depth, columns.size),
+            v_low[pl.ds(first, 2), :, columns].reshape(2 * depth, columns.size),
         )
 
     ladder = half_product(half)
@@ -221,24 +221,33 @@
             high, low = split((driver[block] + part) * weighting[block])
             a_high[block] = high
             a_low[block] = low
-        ladder = half_product(0) + half_product(1)
-    for block in range(n_rep):
-        part = ladder[:, block * depth:(block + 1) * depth]
-        stage[block] = (driver[block] + part) * weighting[block]
-
-    def send_out(step, carry):
-        other = lax.rem(me + step, total)
-        owner = lax.div(other, n_rep)
-        block = lax.rem(other, n_rep)
-        pltpu.make_async_remote_copy(
-            src_ref=stage.at[block, pl.ds(pl.multiple_of(owner * sub, sub), sub)],
-            dst_ref=out_ref.at[pl.ds(pl.multiple_of(wide * row_count + rep * sub, sub), sub)],
-            send_sem=out_send, recv_sem=out_recv,
-            device_id=(owner, block), device_id_type=MESH,
-        ).start()
-        return carry
-
-    lax.fori_loop(1, total, send_out, 0)
+        if sweep < ITERS - 1:
+            ladder = half_product(0) + half_product(1)
+
+    for side in range(2):
+        columns = pl.ds(side * 2 * depth, 2 * depth)
+        ladder = half_product(0, columns) + half_product(1, columns)
+        for near in range(2):
+            block = 2 * side + near
+            part = ladder[:, near * depth:(near + 1) * depth]
+            stage[block] = (driver[block] + part) * weighting[block]
+
+        def send_out(turn, carry):
+            owner = lax.rem(wide + 1 + lax.div(turn, 2), n_wide)
+            block = 2 * side + lax.rem(turn, 2)
+
+            @pl.when(jnp.logical_or(owner != wide, block != rep))
+            def _():
+                pltpu.make_async_remote_copy(
+                    src_ref=stage.at[block, pl.ds(pl.multiple_of(owner * sub, sub), sub)],
+                    dst_ref=out_ref.at[pl.ds(pl.multiple_of(wide * row_count + rep * sub, sub), sub)],
+                    send_sem=out_send, recv_sem=out_recv,
+                    device_id=(owner, block), device_id_type=MESH,
+                ).start()
+
+            return carry
+
+        lax.fori_loop(0, 2 * n_wide, send_out, 0)
     pltpu.make_async_copy(
         stage.at[rep, pl.ds(pl.multiple_of(wide * sub, sub), sub)],
         out_ref.at[pl.ds(pl.multiple_of(wide * row_count + rep * sub, sub), sub)],

time: 23.2 us -> 23.1 us (level)
  no operation moved by 1% of the time
where the time goes in v4:
time: 23.1 us; the launch traced here: 23 us
  Pallas kernels  22.3 us (97%)
  local copies, waits for them, and re-layouts  0.66 us (3%)
    pallas_call x1, Pallas kernels, group_shards(): pl.pallas_call(functools.partial(ladder_kernel, n_wide, n_rep, chunks), o...  22.3 us
    unnamed x1, local copies, waits for them, and re-layouts  0.66 us

profile of v4, /device:TPU:0, one launch (start us, length us, event | category | flops | bytes accessed | tf_op | source)
XLA Modules:
  0.0 23.0 jit_solution(947926118769589999)
XLA Ops:
  0.0 22.3 %ladder_sweeps.1 = f32[256,128]{1,0:T(8,128)S(1)} custom-call(s32[8]{0:T(128)} %count_in.1, s32[8]{0:T(128)} %bitcast.11, f32[128,512]{1,0:T(8,128)} %bitcast.8, f32[256,128]{1,0:T(8,128)} %bitcast.9, f32[8,32]{1,0:T(8,128)} %occ_in.1, f32[8,128]{1,0:T(8,128)} %bitcast.10), custom_call_target="tpu_custom_call" | custom-call | tf_op jit(solution)/shard_map/ladder_sweeps/pallas_call | solution.py:283
  22.3 0.7 %copy.9 = f32[8,32,1,128]{3,2,1,0:T(1,128)} copy(f32[8,32,1,128]{3,2,1,0:T(1,128)S(1)} %bitcast.7) | data formatting | bytes 262144
